TPU v7x, 32 devices: a whole 2x2x4 slice. The times are simulated.
32 devices in a mesh: row: 8 (over z, y), col: 4 (over x, core).
Axes of the slice: x: 2, y: 2, z: 4, core: 2. Of those that a mesh axis runs over, the one named last changes fastest.
Arguments:
- a_blocks: float32 [128, 8, 125, 125], P('row', 'col'), may hold values from -0.1875 to 0.1875
- a_pattern: int32 [128, 8], P('row', 'col'), may hold values 0 or 1
- row_owner: int32 [128], replicated, may hold values from 0 to 127, as said below
- prolong: float32 [8, 24, 125, 125], P('row', 'col'), may hold values from -6 to 6
- p_pattern: int32 [8, 24], P('row', 'col'), may hold values 0 or 1
- prolong_slab: float32 [128, 8, 125, 125], P('row'), may hold values from -0.0625 to 0.0625
Outputs:
- coarse: float32 [8, 24, 125, 125], P('row', 'col')
Inputs may be any that keep to these rules, and one draw needn't show every extreme that they name: row_owner is a permutation; the 16 element-order rows e with e // 16 equal go to at most 2 positions p of any one value p // 16, and exactly 2 for each value they reach.
All inputs are finite; a program needn't handle non-finite values. No bound on the sum of `a_pattern` or of `p_pattern` on one device may be relied on, other than what follows from the above.
Results may differ from a plain program's by a relative error of at most 0.0001.
Values sent between devices are 32-bit elements; how exact they have to be, the bound alone decides.
A program may use at most 128 MiB of HBM per device.

v0:
```python
import functools

import jax
import jax.numpy as jnp
from jax import lax
from jax.experimental import pallas as pl
from jax.experimental.pallas import tpu as pltpu
from jax.sharding import PartitionSpec as P

CAP = 2
Z = 4
L = 128
MESH = pl.DeviceIdType.MESH


def split(v):
    hi = v.astype(jnp.bfloat16)
    lo = (v - hi.astype(jnp.float32)).astype(jnp.bfloat16)
    return hi, lo


def mul3(ah, al, bh, bl):
    dot = functools.partial(jnp.dot, preferred_element_type=jnp.float32)
    return dot(ah, bh) + (dot(ah, bl) + dot(al, bh))


def kernel(
    R, C, a_hbm, s_hbm, p_in, owner, a_pat, p_pat, out,
    a_v, s_v, asend, arecv, stage, sh, sl, ath, atl, macc, mrecv, mfull, mth, mtl, pbuf, ph, plo, total,
    load, a_s, a_r, m_s, m_r, g_s, g_r, u_s, u_r, d_s, d_r, y_s, y_r,
):
    W, KP, B = a_v.shape[0], a_v.shape[1], a_v.shape[2]
    NA, NJ = s_v.shape[1] // B, p_in.shape[0]
    Y = R // Z
    me, col = lax.axis_index("row"), lax.axis_index("col")
    z, y = lax.div(me, Y), lax.rem(me, Y)

    load_a = pltpu.make_async_copy(a_hbm, a_v, load.at[0])
    load_s = pltpu.make_async_copy(s_hbm, s_v, load.at[1])
    load_a.start()
    load_s.start()

    barrier = pltpu.get_barrier_semaphore()
    for i in range(1, R):
        pl.semaphore_signal(barrier, inc=1, device_id={"row": lax.rem(me + i, R)}, device_id_type=MESH)
    for i in range(1, C):
        pl.semaphore_signal(barrier, inc=1, device_id={"col": lax.rem(col + i, C)}, device_id_type=MESH)

    pl.semaphore_wait(barrier, R + C - 2)

    def p_copy(slot, target, s_sem, r_sem):
        return pltpu.make_async_remote_copy(
            src_ref=pbuf.at[slot], dst_ref=pbuf.at[slot], send_sem=s_sem, recv_sem=r_sem,
            device_id={"row": target}, device_id_type=MESH,
        )

    def up(t):
        return p_copy((z - t) * Y + y, me + Y, u_s.at[t], u_r.at[t + 1])

    def down(t):
        return p_copy((z + t) * Y + y, me - Y, d_s.at[t], d_r.at[t + 1])

    def across(zo, i):
        return p_copy(zo * Y + y, z * Y + lax.rem(y + i, Y), y_s.at[zo * Y + i], y_r.at[zo * Y + i])

    def hop(t):
        @pl.when(z >= t)
        def _():
            if t > 0:
                p_copy((z - t) * Y + y, me, u_s.at[t], u_r.at[t]).wait_recv()

            @pl.when(z < Z - 1)
            def _():
                up(t).start()

            for i in range(1, Y):
                across(z - t, i).start()

        @pl.when(z + t < Z)
        def _():
            if t > 0:
                p_copy((z + t) * Y + y, me, d_s.at[t], d_r.at[t]).wait_recv()

            @pl.when(z > 0)
            def _():
                down(t).start()

            if t > 0:
                for i in range(1, Y):
                    across(z + t, i).start()


    def pair(source, target):
        first, last = jnp.int32(W), jnp.int32(-1)
        for e in range(W):
            hit = lax.div(owner[source * W + e], W) == target
            first = jnp.minimum(first, jnp.where(hit, e, W))
            last = jnp.maximum(last, jnp.where(hit, e, -1))
        valid = last >= 0
        return (jnp.where(valid, first, 0), jnp.where(valid, last, 0)), valid

    def a_copy(step):
        return pltpu.make_async_remote_copy(
            src_ref=asend.at[step], dst_ref=arecv.at[step], send_sem=a_s.at[step], recv_sem=a_r.at[step],
            device_id={"row": lax.rem(me + step, R)}, device_id_type=MESH,
        )

    def pack(buf, step):
        rows, valid = pair(me, lax.rem(me + step, R))
        for s in range(CAP):
            for k in range(KP):
                scale = jnp.where(valid, a_pat[k, rows[s]], 0).astype(jnp.float32)
                buf[step, s, k] = jnp.zeros((L, L), jnp.float32)
                buf[step, s, k, 0:B, 0:B] = a_v[rows[s], k] * scale

    def step_of(j):
        half = lax.div(j + 1, 2)
        return R // 2 + half * (1 - 2 * lax.rem(j, 2))

    load_a.wait()

    def send_step(j, carry):
        step = step_of(j)
        pack(asend, step)
        a_copy(step).start()
        return carry

    lax.fori_loop(0, R - 1, send_step, 0)
    for n in range(NJ):
        pbuf[me, n] = jnp.zeros((L, L), jnp.float32)
        pbuf[me, n, 0:B, 0:B] = p_in[n, :, 0, :] * p_pat[0, n].astype(jnp.float32)
    hop(0)
    pack(arecv, 0)
    stage[...] = jnp.zeros_like(stage)
    macc[...] = jnp.zeros_like(macc)
    load_s.wait()

    def m_copy(step):
        target = lax.rem(me + step, R)
        return pltpu.make_async_remote_copy(
            src_ref=macc.at[target], dst_ref=mrecv.at[step], send_sem=m_s.at[step], recv_sem=m_r.at[step],
            device_id={"row": target}, device_id_type=MESH,
        )

    def work(step, arrives, last=False):
        source = lax.rem(me - step + R, R)
        rows, valid = pair(source, me)
        for s in range(CAP):
            g = jnp.where(valid, owner[source * W + rows[s]] - me * W, 0)

            def slab(b, carry):
                for h in range(2):
                    stage[2 * b + h, 0:B, 0:B] = s_v[g, pl.ds(2 * b + h, B, stride=NA), :]
                for h in range(2):
                    hi, lo = split(stage[2 * b + h])
                    sh[b, s * L : (s + 1) * L, h * L : (h + 1) * L] = hi
                    sl[b, s * L : (s + 1) * L, h * L : (h + 1) * L] = lo
                return carry

            lax.fori_loop(0, NA // 2, slab, 0)
        if arrives:
            a_copy(step).wait_recv()
        for s in range(CAP):
            for k in range(KP):
                hi, lo = split(arecv[step, s, k].T)
                ath[k * L : (k + 1) * L, s * L : (s + 1) * L] = hi
                atl[k * L : (k + 1) * L, s * L : (s + 1) * L] = lo

        def add(i, carry):
            b = lax.rem(i + lax.div(me, 2), NA // 2)
            r = mul3(ath[...], atl[...], sh[b], sl[b])
            macc[2 * b] += r[:, 0:L]
            macc[2 * b + 1] += r[:, L : 2 * L]
            for h in range(2 if last else 0):
                @pl.when(2 * b + h != me)
                def _():
                    m_copy(lax.rem(2 * b + h - me + R, R)).start()
            return carry

        lax.fori_loop(0, NA // 2, add, 0)

    def remote_step(j, carry):
        work(step_of(j), True)
        return carry

    work(0, False)
    at = 0
    for t in range(1, Z):
        hop(t)
        until = (R - 1) * t // Z if t < Z - 1 else R - 2
        lax.fori_loop(at, until, remote_step, 0)
        at = until
    work(step_of(jnp.int32(R - 2)), True, last=True)

    for zo in range(Z):
        for i in range(1, Y):
            across(zo, i).wait_recv()

    def p_split(r, carry):
        for n in range(NJ):
            hi, lo = split(pbuf[r, n])
            at = pl.ds(pl.multiple_of(r * L, L), L)
            ph[at, n * L : (n + 1) * L] = hi
            plo[at, n * L : (n + 1) * L] = lo
        return carry

    lax.fori_loop(0, R, p_split, 0)

    mfull[col] = macc[me]

    def m_add(j, carry):
        step = step_of(j)
        m_copy(step).wait_recv()
        mfull[col] += mrecv[step]
        return carry

    lax.fori_loop(0, R - 1, m_add, 0)

    def g_copy(i):
        return pltpu.make_async_remote_copy(
            src_ref=mfull.at[col], dst_ref=mfull.at[col], send_sem=g_s.at[i], recv_sem=g_r.at[i],
            device_id={"col": lax.rem(col + i, C)}, device_id_type=MESH,
        )

    for i in range(1, C):
        g_copy(i).start()
    total[...] = jnp.zeros_like(total)

    for i in range(C):
        source = lax.rem(col - i + C, C)
        if i > 0:
            g_copy(i).wait_recv()
        for k in range(KP):
            hi, lo = split(mfull[source, k * L : (k + 1) * L, :].T)
            mth[:, k * L : (k + 1) * L] = hi
            mtl[:, k * L : (k + 1) * L] = lo
        rows = pl.ds(pl.multiple_of(source * KP * L, KP * L), KP * L)
        total[...] += mul3(mth[...], mtl[...], ph[rows, :], plo[rows, :])

    for n in range(NJ):
        out[0, n] = total[0:B, n * L : n * L + B]

    def a_done(j, carry):
        a_copy(j + 1).wait_send()
        m_copy(j + 1).wait_send()
        return carry

    lax.fori_loop(0, R - 1, a_done, 0)
    for i in range(1, C):
        g_copy(i).wait_send()
    for t in range(Z):
        @pl.when((z >= t) & (z < Z - 1))
        def _():
            up(t).wait_send()

        @pl.when((z + t < Z) & (z > 0))
        def _():
            down(t).wait_send()

    for zo in range(Z):
        for i in range(1, Y):
            across(zo, i).wait_send()


def shards(a_blocks, a_pattern, row_owner, prolong, p_pattern, prolong_slab):
    R, C = lax.axis_size("row"), lax.axis_size("col")
    W, KP, B = a_blocks.shape[:3]
    NA, NJ = prolong_slab.shape[1], prolong.shape[1]
    f32, bf16 = jnp.float32, jnp.bfloat16
    slab = prolong_slab.transpose(0, 2, 1, 3).reshape(W, B * NA, B)
    dma = pltpu.SemaphoreType.DMA
    vmem = pl.BlockSpec(memory_space=pltpu.VMEM)
    smem = pl.BlockSpec(memory_space=pltpu.SMEM)
    hbm = pl.BlockSpec(memory_space=pl.ANY)
    return pl.pallas_call(
        functools.partial(kernel, R, C),
        out_shape=jax.ShapeDtypeStruct((1, NJ, B, B), f32),
        in_specs=[hbm, hbm, vmem, smem, smem, smem],
        out_specs=vmem,
        scratch_shapes=[
            pltpu.VMEM((W, KP, B, B), f32),
            pltpu.VMEM((W, B * NA, B), f32),
            pltpu.VMEM((R, CAP, KP, L, L), f32),
            pltpu.VMEM((R, CAP, KP, L, L), f32),
            pltpu.VMEM((NA, L, L), f32),
            pltpu.VMEM((NA // 2, CAP * L, 2 * L), bf16),
            pltpu.VMEM((NA // 2, CAP * L, 2 * L), bf16),
            pltpu.VMEM((KP * L, CAP * L), bf16),
            pltpu.VMEM((KP * L, CAP * L), bf16),
            pltpu.VMEM((NA, KP * L, L), f32),
            pltpu.VMEM((R, KP * L, L), f32),
            pltpu.VMEM((C, KP * L, L), f32),
            pltpu.VMEM((L, KP * L), bf16),
            pltpu.VMEM((L, KP * L), bf16),
            pltpu.VMEM((R, NJ, L, L), f32),
            pltpu.VMEM((R * L, NJ * L), bf16),
            pltpu.VMEM((R * L, NJ * L), bf16),
            pltpu.VMEM((L, NJ * L), f32),
            dma((2,)),
            dma((R,)), dma((R,)), dma((R,)), dma((R,)), dma((C,)), dma((C,)),
            dma((Z,)), dma((Z + 1,)), dma((Z,)), dma((Z + 1,)), dma((R,)), dma((R,)),
        ],
        compiler_params=pltpu.CompilerParams(
            collective_id=0, has_side_effects=True, vmem_limit_bytes=58 * 1024 * 1024
        ),
    )(a_blocks, slab, prolong.transpose(1, 2, 0, 3), row_owner, a_pattern.T, p_pattern)


def solution(mesh):
    in_specs = (
        P("row", "col", None, None),
        P("row", "col"),
        P(),
        P("row", "col", None, None),
        P("row", "col"),
        P("row", None, None, None),
    )
    out_specs = P("row", "col", None, None)
    return jax.shard_map(shards, mesh=mesh, in_specs=in_specs, out_specs=out_specs, check_vma=False)
```

profile of v0, /device:TPU:13, one launch (start us, length us, event | category | flops | bytes accessed | tf_op | source)
XLA Modules:
  0.0 114.9 jit_solution(11708208031197909699)
XLA Ops:
  0.0 3.2 %copy.7.a_hbm = f32[16,2,125,125]{3,2,1,0:T(8,128)} copy(f32[16,2,125,125]{3,1,2,0:T(2,128)} %param.6) | data formatting | bytes 4000000 | tf_op args[0]
  3.2 109.6 %shard_map.64 = f32[1,6,125,125]{3,2,1,0:T(8,128)} custom-call(f32[16,2,125,125]{3,2,1,0:T(8,128)} %copy.7.a_hbm, f32[16,1000,125]{2,1,0:T(8,128)} %bitcast.5, f32[6,125,1,125]{3,2,1,0:T(1,128)} %bitcast.6, s32[128]{0:T(128)} %owner.1, s32[2,16]{1,0:T(2,128)} %bitcast.7, s32[1,6]{1,0:T(1,128)} %p_pat.1), custom_call_target="tpu_custom_call" | custom-call | tf_op jit(solution)/shard_map/pallas_call | solution.py:275
  112.8 2.1 %copy.8 = f32[1,6,125,125]{3,0,2,1:T(1,128)} copy(f32[1,6,125,125]{3,2,1,0:T(8,128)} %shard_map.64) | data formatting | bytes 750000 | tf_op jit(solution)/shard_map/pallas_call | solution.py:275
where the time goes:
time: 115 us
  Pallas kernels  110 us (96%)
  local copies, waits for them, and re-layouts  5.33 us (5%)
    pallas_call x1, Pallas kernels, shards(): pl.pallas_call(functools.partial(kernel, R, C), out_shape=jax.ShapeDtypeS...  110 us
    unnamed x1, local copies, waits for them, and re-layouts  3.2 us

commit v1 on v0

v1 whole, which is shorter than its diff:
```python
import functools

import jax
import jax.numpy as jnp
from jax import lax
from jax.experimental import pallas as pl
from jax.experimental.pallas import tpu as pltpu
from jax.sharding import PartitionSpec as P

CAP = 2
Z = 4
L = 128
WAVES = 4
PARTS = 2
MESH = pl.DeviceIdType.MESH
VMEM_LIMIT = 58 * 1024 * 1024

P_NEAR = (0, 3)
P_FAR = ((0, 0), (0, 0))
P_IN = ((2, 1), (2, 3))
P_OUT = ((2, 5), (3, 1))


def split(v):
    hi = v.astype(jnp.bfloat16)
    lo = (v - hi.astype(jnp.float32)).astype(jnp.bfloat16)
    return hi, lo


def dot(a, b):
    return jnp.dot(a, b, preferred_element_type=jnp.float32)


def kernel(
    R, C, KEEP, a_hbm, s_hbm, p_in, owner, a_pat, p_pat, out,
    a_v, s_v, flip, asend, arecv, stage, sh, sl, ahl, macc, yrecv, nbuf, frecv, nrecv, crecv,
    mfull, mth, mtl, pbuf, ph, plo, total,
    load, a_s, a_r, y_s, y_r, f_s, f_r, n_s, n_r, c_s, c_r, g_s, g_r, pn_s, pf_s, pw_s, py_s, p_r,
):
    KP, W, B = a_pat.shape[0], a_pat.shape[1], a_v.shape[1]
    NA, NJ = s_v.shape[1] // B, p_in.shape[0]
    NV, RV = WAVES, KP * L // WAVES
    H, Q = L // RV, NJ // PARTS
    Y = R // Z
    f32 = jnp.float32
    me, col = lax.axis_index("row"), lax.axis_index("col")
    z, y = lax.div(me, Y), lax.rem(me, Y)
    near0 = 2 * lax.div(z, 2)
    far0 = 2 - near0
    zn = 2 * near0 + 1 - z
    inner = (z == 1) | (z == 2)
    far_inner = jnp.where(z < 2, 2, 1)

    load_a = pltpu.make_async_copy(a_hbm, a_v, load.at[0])
    load_s = pltpu.make_async_copy(s_hbm, s_v, load.at[1])
    load_a.start()
    load_s.start()

    barrier = pltpu.get_barrier_semaphore()
    for i in range(1, R):
        pl.semaphore_signal(barrier, inc=1, device_id={"row": lax.rem(me + i, R)}, device_id_type=MESH)
    for i in range(1, C):
        pl.semaphore_signal(barrier, inc=1, device_id={"col": lax.rem(col + i, C)}, device_id_type=MESH)

    def pair(source, target):
        first, last = jnp.int32(W), jnp.int32(-1)
        for e in range(W):
            hit = lax.div(owner[source * W + e], W) == target
            first = jnp.minimum(first, jnp.where(hit, e, W))
            last = jnp.maximum(last, jnp.where(hit, e, -1))
        valid = last >= 0
        return (jnp.where(valid, first, 0), jnp.where(valid, last, 0)), valid

    def step_of(j):
        half = lax.div(j + 1, 2)
        return R // 2 + half * (1 - 2 * lax.rem(j, 2))

    def a_copy(v, step):
        return pltpu.make_async_remote_copy(
            src_ref=asend.at[v, step], dst_ref=arecv.at[v, step], send_sem=a_s.at[v, step], recv_sem=a_r.at[v, step],
            device_id={"row": lax.rem(me + step, R)}, device_id_type=MESH,
        )

    def pack(buf, step, k):
        rows, valid = pair(me, lax.rem(me + step, R))
        for s in range(CAP):
            scale = jnp.where(valid, a_pat[k, rows[s]], 0).astype(f32)
            flip[s, 0:B, 0:B] = a_v[pl.ds(rows[s] * (B * KP) + k, B, stride=KP), :] * scale
        for s in range(CAP):
            turned = flip[s].T
            for h in range(H):
                buf[k * H + h, step, s] = turned[h * RV : (h + 1) * RV]

    def p_copy(slot, q, target, s_sem):
        at = pl.ds(q * Q, Q)
        return pltpu.make_async_remote_copy(
            src_ref=pbuf.at[slot, at], dst_ref=pbuf.at[slot, at], send_sem=s_sem, recv_sem=p_r.at[slot, q],
            device_id={"row": target}, device_id_type=MESH,
        )

    def p_near(q):
        return p_copy(me, q, zn * Y + y, pn_s.at[q])

    def p_far(q):
        return p_copy(me, q, far_inner * Y + y, pf_s.at[q])

    def p_forward(u, q):
        return p_copy((far0 + u) * Y + y, q, zn * Y + y, pw_s.at[u, q])

    def p_across(zo, i, q):
        return p_copy(zo * Y + y, q, z * Y + lax.rem(y + i, Y), py_s.at[zo, i, q])

    def p_arrived(slot, q):
        p_copy(slot, q, me, pn_s.at[q]).wait_recv()

    def all_across(zo, q):
        for i in range(1, Y):
            p_across(zo, i, q).start()

    def near_arrives(q):
        p_arrived(zn * Y + y, q)
        all_across(zn, q)

    def far_arrives(q):
        for u in range(2):
            p_arrived((far0 + u) * Y + y, q)

            @pl.when(inner)
            def _():
                p_forward(u, q).start()

            all_across(far0 + u, q)

    def y_copy(v, i, h):
        target = lax.rem(y + i, Y)
        at = pl.ds(near0 if h else far0, 2)
        return pltpu.make_async_remote_copy(
            src_ref=macc.at[v, target, at], dst_ref=yrecv.at[v, i, at], send_sem=y_s.at[v, i, h], recv_sem=y_r.at[v, i, h],
            device_id={"row": z * Y + target}, device_id_type=MESH,
        )

    def f_copy(v):
        return pltpu.make_async_remote_copy(
            src_ref=nbuf.at[v, pl.ds(far0, 2)], dst_ref=frecv.at[v], send_sem=f_s.at[v], recv_sem=f_r.at[v],
            device_id={"row": zn * Y + y}, device_id_type=MESH,
        )

    def n_copy(v):
        return pltpu.make_async_remote_copy(
            src_ref=nbuf.at[v, zn], dst_ref=nrecv.at[v], send_sem=n_s.at[v], recv_sem=n_r.at[v],
            device_id={"row": zn * Y + y}, device_id_type=MESH,
        )

    def c_copy(v, u):
        return pltpu.make_async_remote_copy(
            src_ref=nbuf.at[v, far0 + u], dst_ref=crecv.at[v], send_sem=c_s.at[v, u], recv_sem=c_r.at[v],
            device_id={"row": (far0 + u) * Y + y}, device_id_type=MESH,
        )

    def g_copy(v, i):
        at = pl.ds(pl.multiple_of(col * RV, RV), RV)
        return pltpu.make_async_remote_copy(
            src_ref=mfull.at[v, at], dst_ref=mfull.at[v, at], send_sem=g_s.at[v, i], recv_sem=g_r.at[v, i],
            device_id={"col": lax.rem(col + i, C)}, device_id_type=MESH,
        )

    def over_y(v):
        for h in range(2):
            for i in range(1, Y):
                y_copy(v, i, h).start()

    def over_near(v):
        for h in range(2):
            at = pl.ds(near0 if h else far0, 2)
            acc = macc[v, y, at]
            for i in range(1, Y):
                y_copy(v, i, h).wait_recv()
                acc += yrecv[v, i, at]
            nbuf[v, at] = acc
            if h == 0:
                @pl.when(jnp.logical_not(inner))
                def _():
                    f_copy(v).start()
            else:
                n_copy(v).start()

    def over_middle(v):
        @pl.when(inner)
        def _():
            f_copy(v).wait_recv()
            nbuf[v, pl.ds(far0, 2)] += frecv[v]
            for u in range(2):
                c_copy(v, u).start()

    def over_col(v):
        n_copy(v).wait_recv()
        c_copy(v, 0).wait_recv()
        mfull[v, pl.ds(pl.multiple_of(col * RV, RV), RV)] = nbuf[v, z] + nrecv[v] + crecv[v]
        for i in range(1, C):
            g_copy(v, i).start()

    def last_product(v):
        for i in range(1, C):
            g_copy(v, i).wait_recv()
        for c in range(C * RV // L):
            hi, lo = split(mfull[v, c * L : (c + 1) * L].T)
            mth[:, c * L : (c + 1) * L] = hi
            mtl[:, c * L : (c + 1) * L] = lo
        total[...] += dot(mth[...], ph[v]) + (dot(mth[...], plo[v]) + dot(mtl[...], ph[v]))

    flip[...] = jnp.zeros_like(flip)
    load_a.wait()

    def first_pack(j, carry):
        pack(asend, step_of(j), 0)
        return carry

    lax.fori_loop(0, R - 1, first_pack, 0)
    pl.semaphore_wait(barrier, R + C - 2)

    for v in range(H):
        def send(j, carry):
            a_copy(v, step_of(j)).start()
            return carry

        lax.fori_loop(0, R - 1, send, 0)

    for k in range(1, KP):
        def pack_send(j, carry):
            step = step_of(j)
            pack(asend, step, k)
            a_copy(k * H, step).start()
            return carry

        lax.fori_loop(0, R - 1, pack_send, 0)
        for h in range(1, H):
            def send_rest(j, carry):
                a_copy(k * H + h, step_of(j)).start()
                return carry

            lax.fori_loop(0, R - 1, send_rest, 0)

    for n in range(NJ):
        pbuf[me, n] = jnp.zeros((L, L), f32)
        pbuf[me, n, 0:B, 0:B] = p_in[n, :, 0, :] * p_pat[0, n].astype(f32)
    for q in range(PARTS):
        p_near(q).start()
        all_across(z, q)
    for k in range(KP):
        pack(arecv, 0, k)
    stage[...] = jnp.zeros_like(stage)
    macc[...] = jnp.zeros_like(macc)
    total[...] = jnp.zeros_like(total)
    load_s.wait()

    def slab(step, keep):
        source = lax.rem(me - step + R, R)
        rows, valid = pair(source, me)
        for s in range(CAP):
            g = jnp.where(valid, owner[source * W + rows[s]] - me * W, 0)

            def one(b, carry):
                for h in range(2):
                    stage[2 * b + h, 0:B, 0:B] = s_v[g, pl.ds(2 * b + h, B, stride=NA), :]
                for h in range(2):
                    hi, lo = split(stage[2 * b + h])
                    sh[keep, b, s * L : (s + 1) * L, h * L : (h + 1) * L] = hi
                    sl[keep, b, s * L : (s + 1) * L, h * L : (h + 1) * L] = lo
                return carry

            lax.fori_loop(0, NA // 2, one, 0)

    def work(t, carry):
        v, j = lax.div(t, R), lax.rem(t, R)
        step = jnp.where(j == 0, 0, step_of(j - 1))
        keep = step if KEEP else 0
        if KEEP:
            @pl.when(v == 0)
            def _():
                slab(step, step)
        else:
            slab(step, 0)

        @pl.when(j > 0)
        def _():
            a_copy(v, step).wait_recv()

        for s in range(CAP):
            hi, lo = split(arecv[v, step, s])
            ahl[0:RV, s * L : (s + 1) * L] = hi
            ahl[RV : 2 * RV, s * L : (s + 1) * L] = lo
        for b in range(NA // 2):
            both = dot(ahl[...], sh[keep, b])
            r = both[0:RV] + (both[RV : 2 * RV] + dot(ahl[0:RV], sl[keep, b]))
            for h in range(2):
                a = 2 * b + h
                macc[v, a % Y, a // Y] += r[:, h * L : (h + 1) * L]

        def at(when, act):
            @pl.when((v == when[0]) & (j == when[1]))
            def _():
                act()

        def chain(when, act):
            @pl.when((v > 0) & (j == when))
            def _():
                act(v - 1)

        @pl.when(j == R - 1)
        def _():
            over_y(v)

        chain(R // 2 - 2, over_near)
        chain(R // 2, over_middle)
        chain(R // 2 + 2, over_col)
        for q in range(PARTS):
            at(P_FAR[q], lambda q=q: p_far(q).start())
            at(P_NEAR, lambda q=q: near_arrives(q))

            @pl.when(inner)
            def _():
                at(P_IN[q], lambda q=q: far_arrives(q))

            @pl.when(jnp.logical_not(inner))
            def _():
                at(P_OUT[q], lambda q=q: far_arrives(q))
        return carry

    lax.fori_loop(0, NV * R, work, 0)

    for q in range(PARTS):
        for zo in range(Z):
            for i in range(1, Y):
                p_arrived(zo * Y + lax.rem(y + i, Y), q)

    def p_split(r, carry):
        c, k = lax.div(r, KP), lax.rem(r, KP)
        at = pl.ds(pl.multiple_of(c * RV, RV), RV)
        for n in range(NJ):
            hi, lo = split(pbuf[r, n])
            for h in range(H):
                ph[k * H + h, at, n * L : (n + 1) * L] = hi[h * RV : (h + 1) * RV]
                plo[k * H + h, at, n * L : (n + 1) * L] = lo[h * RV : (h + 1) * RV]
        return carry

    lax.fori_loop(0, R, p_split, 0)
    for v in range(NV - 1):
        last_product(v)
    over_near(NV - 1)
    over_middle(NV - 1)
    over_col(NV - 1)
    last_product(NV - 1)

    for n in range(NJ):
        out[0, n] = total[0:B, n * L : n * L + B]

    def sent(v, carry):
        def one(j, carry):
            a_copy(v, j + 1).wait_send()
            return carry

        lax.fori_loop(0, R - 1, one, 0)
        for i in range(1, Y):
            for h in range(2):
                y_copy(v, i, h).wait_send()
        n_copy(v).wait_send()

        @pl.when(inner)
        def _():
            for u in range(2):
                c_copy(v, u).wait_send()

        @pl.when(jnp.logical_not(inner))
        def _():
            f_copy(v).wait_send()

        for i in range(1, C):
            g_copy(v, i).wait_send()
        return carry

    lax.fori_loop(0, NV, sent, 0)
    for q in range(PARTS):
        p_near(q).wait_send()
        p_far(q).wait_send()

        @pl.when(inner)
        def _():
            for u in range(2):
                p_forward(u, q).wait_send()

        for zo in range(Z):
            for i in range(1, Y):
                p_across(zo, i, q).wait_send()


def shards(a_blocks, a_pattern, row_owner, prolong, p_pattern, prolong_slab):
    R, C = lax.axis_size("row"), lax.axis_size("col")
    W, KP, B = a_blocks.shape[:3]
    NA, NJ = prolong_slab.shape[1], prolong.shape[1]
    f32, bf16 = jnp.float32, jnp.bfloat16
    Y, NV, RV = R // Z, WAVES, KP * L // WAVES
    keep = R * NA <= 64
    slots = R if keep else 1
    oper = a_blocks.transpose(0, 2, 1, 3).reshape(W * B * KP, B)
    slab = prolong_slab.transpose(0, 2, 1, 3).reshape(W, B * NA, B)
    dma = pltpu.SemaphoreType.DMA
    vmem = pl.BlockSpec(memory_space=pltpu.VMEM)
    smem = pl.BlockSpec(memory_space=pltpu.SMEM)
    hbm = pl.BlockSpec(memory_space=pl.ANY)
    return pl.pallas_call(
        functools.partial(kernel, R, C, keep),
        out_shape=jax.ShapeDtypeStruct((1, NJ, B, B), f32),
        in_specs=[hbm, hbm, vmem, smem, smem, smem],
        out_specs=vmem,
        scratch_shapes=[
            pltpu.VMEM((W * B * KP, B), f32),
            pltpu.VMEM((W, B * NA, B), f32),
            pltpu.VMEM((CAP, L, L), f32),
            pltpu.VMEM((NV, R, CAP, RV, L), f32),
            pltpu.VMEM((NV, R, CAP, RV, L), f32),
            pltpu.VMEM((NA, L, L), f32),
            pltpu.VMEM((slots, NA // 2, CAP * L, 2 * L), bf16),
            pltpu.VMEM((slots, NA // 2, CAP * L, 2 * L), bf16),
            pltpu.VMEM((2 * RV, CAP * L), bf16),
            pltpu.VMEM((NV, Y, Z, RV, L), f32),
            pltpu.VMEM((NV, Y, Z, RV, L), f32),
            pltpu.VMEM((NV, Z, RV, L), f32),
            pltpu.VMEM((NV, 2, RV, L), f32),
            pltpu.VMEM((NV, RV, L), f32),
            pltpu.VMEM((NV, RV, L), f32),
            pltpu.VMEM((NV, C * RV, L), f32),
            pltpu.VMEM((L, C * RV), bf16),
            pltpu.VMEM((L, C * RV), bf16),
            pltpu.VMEM((R, NJ, L, L), f32),
            pltpu.VMEM((NV, C * RV, NJ * L), bf16),
            pltpu.VMEM((NV, C * RV, NJ * L), bf16),
            pltpu.VMEM((L, NJ * L), f32),
            dma((2,)),
            dma((NV, R)), dma((NV, R)),
            dma((NV, Y, 2)), dma((NV, Y, 2)),
            dma((NV,)), dma((NV,)), dma((NV,)), dma((NV,)),
            dma((NV, 2)), dma((NV,)),
            dma((NV, C)), dma((NV, C)),
            dma((PARTS,)), dma((PARTS,)), dma((2, PARTS)), dma((Z, Y, PARTS)), dma((R, PARTS)),
        ],
        compiler_params=pltpu.CompilerParams(
            collective_id=0, has_side_effects=True, vmem_limit_bytes=VMEM_LIMIT
        ),
    )(oper, slab, prolong.transpose(1, 2, 0, 3), row_owner, a_pattern.T, p_pattern)


def solution(mesh):
    in_specs = (
        P("row", "col", None, None),
        P("row", "col"),
        P(),
        P("row", "col", None, None),
        P("row", "col"),
        P("row", None, None, None),
    )
    out_specs = P("row", "col", None, None)
    return jax.shard_map(shards, mesh=mesh, in_specs=in_specs, out_specs=out_specs, check_vma=False)
```

time: 115 us -> 119 us (1.035)
  the two profiles are of different devices: /device:TPU:13 before, /device:TPU:0 now
where the time goes in v1:
time: 119 us
  Pallas kernels  117 us (98%)
  local copies, waits for them, and re-layouts  2.13 us (2%)
    pallas_call x1, Pallas kernels, shards(): pl.pallas_call(functools.partial(kernel, R, C, keep), out_shape=jax.Shape...  117 us

profile of v1, /device:TPU:0, one launch (start us, length us, event | category | flops | bytes accessed | tf_op | source)
XLA Modules:
  0.0 119.3 jit_solution(16176957594652873346)
XLA Ops:
  0.0 117.1 %shard_map.64 = f32[1,6,125,125]{3,2,1,0:T(8,128)} custom-call(f32[4000,125]{1,0:T(8,128)} %bitcast.9, f32[16,1000,125]{2,1,0:T(8,128)} %bitcast.8, f32[6,125,1,125]{3,2,1,0:T(1,128)} %bitcast.10, s32[128]{0:T(128)} %owner.1, s32[2,16]{1,0:T(2,128)} %bitcast.11, s32[1,6]{1,0:T(1,128)} %p_pat.1), custom_call_target="tpu_custom_call" | custom-call | tf_op jit(solution)/shard_map/pallas_call | solution.py:410
  117.1 2.1 %copy.7 = f32[1,6,125,125]{3,0,2,1:T(1,128)} copy(f32[1,6,125,125]{3,2,1,0:T(8,128)} %shard_map.64) | data formatting | bytes 750000 | tf_op jit(solution)/shard_map/pallas_call | solution.py:410

commit v2 on v1

--- a/solution.py
+++ b/solution.py
@@ -11,14 +11,18 @@
 Z = 4
 L = 128
 WAVES = 4
-PARTS = 2
+PARTS = 3
+WINDOW = 0.25
+DIRECT = 1
 MESH = pl.DeviceIdType.MESH
 VMEM_LIMIT = 58 * 1024 * 1024
 
-P_NEAR = (0, 3)
-P_FAR = ((0, 0), (0, 0))
-P_IN = ((2, 1), (2, 3))
-P_OUT = ((2, 5), (3, 1))
+SUMS = (0.2, 0.4, 0.6)
+OWN = 0.02
+NEAR = 0.3
+FAR = (0.25, 0.75)
+INTO = 0.31
+ONWARD = 0.12
 
 
 def split(v):
@@ -33,9 +37,9 @@
 
 def kernel(
     R, C, KEEP, a_hbm, s_hbm, p_in, owner, a_pat, p_pat, out,
-    a_v, s_v, flip, asend, arecv, stage, sh, sl, ahl, macc, yrecv, nbuf, frecv, nrecv, crecv,
+    a_v, s_v, flip, asend, arecv, stage, sh, sl, ahl, macc, yrecv, nbuf, frecv, nrecv, crecv, mrecv,
     mfull, mth, mtl, pbuf, ph, plo, total,
-    load, a_s, a_r, y_s, y_r, f_s, f_r, n_s, n_r, c_s, c_r, g_s, g_r, pn_s, pf_s, pw_s, py_s, p_r,
+    load, a_s, a_r, y_s, y_r, f_s, f_r, n_s, n_r, c_s, c_r, m_s, m_r, g_s, g_r, pn_s, pf_s, pw_s, py_s, p_r,
 ):
     KP, W, B = a_pat.shape[0], a_pat.shape[1], a_v.shape[1]
     NA, NJ = s_v.shape[1] // B, p_in.shape[0]
@@ -199,6 +203,31 @@
         for i in range(1, C):
             g_copy(v, i).start()
 
+    def m_copy(v, step):
+        target = lax.rem(me + step, R)
+        d = jnp.maximum(v - (NV - DIRECT), 0)
+        return pltpu.make_async_remote_copy(
+            src_ref=macc.at[v, lax.rem(target, Y), lax.div(target, Y)], dst_ref=mrecv.at[d, step],
+            send_sem=m_s.at[d, step], recv_sem=m_r.at[d, step],
+            device_id={"row": target}, device_id_type=MESH,
+        )
+
+    def over_rows(v):
+        def one(j, carry):
+            m_copy(v, step_of(j)).start()
+            return carry
+
+        lax.fori_loop(0, R - 1, one, 0)
+
+    def col_after_rows(v):
+        acc = macc[v, y, z]
+        for step in range(1, R):
+            m_copy(v, step).wait_recv()
+            acc += mrecv[v - (NV - DIRECT), step]
+        mfull[v, pl.ds(pl.multiple_of(col * RV, RV), RV)] = acc
+        for i in range(1, C):
+            g_copy(v, i).start()
+
     def last_product(v):
         for i in range(1, C):
             g_copy(v, i).wait_recv()
@@ -218,34 +247,23 @@
     lax.fori_loop(0, R - 1, first_pack, 0)
     pl.semaphore_wait(barrier, R + C - 2)
 
-    for v in range(H):
-        def send(j, carry):
-            a_copy(v, step_of(j)).start()
+    def send(n, carry):
+        a_copy(lax.div(n, R - 1), step_of(lax.rem(n, R - 1))).start()
+        return carry
+
+    window = min(int(WINDOW * NV * R), H * (R - 1))
+    lax.fori_loop(0, window, send, 0)
+
+    for k in range(1, KP):
+        def later_pack(j, carry):
+            pack(asend, step_of(j), k)
             return carry
 
-        lax.fori_loop(0, R - 1, send, 0)
-
-    for k in range(1, KP):
-        def pack_send(j, carry):
-            step = step_of(j)
-            pack(asend, step, k)
-            a_copy(k * H, step).start()
-            return carry
-
-        lax.fori_loop(0, R - 1, pack_send, 0)
-        for h in range(1, H):
-            def send_rest(j, carry):
-                a_copy(k * H + h, step_of(j)).start()
-                return carry
-
-            lax.fori_loop(0, R - 1, send_rest, 0)
+        lax.fori_loop(0, R - 1, later_pack, 0)
 
     for n in range(NJ):
         pbuf[me, n] = jnp.zeros((L, L), f32)
         pbuf[me, n, 0:B, 0:B] = p_in[n, :, 0, :] * p_pat[0, n].astype(f32)
-    for q in range(PARTS):
-        p_near(q).start()
-        all_across(z, q)
     for k in range(KP):
         pack(arecv, 0, k)
     stage[...] = jnp.zeros_like(stage)
@@ -284,6 +302,11 @@
         @pl.when(j > 0)
         def _():
             a_copy(v, step).wait_recv()
+            ahead = v * (R - 1) + j - 1 + window
+
+            @pl.when(ahead < NV * (R - 1))
+            def _():
+                send(ahead, 0)
 
         for s in range(CAP):
             hi, lo = split(arecv[v, step, s])
@@ -296,37 +319,48 @@
                 a = 2 * b + h
                 macc[v, a % Y, a // Y] += r[:, h * L : (h + 1) * L]
 
-        def at(when, act):
-            @pl.when((v == when[0]) & (j == when[1]))
-            def _():
-                act()
-
-        def chain(when, act):
-            @pl.when((v > 0) & (j == when))
-            def _():
-                act(v - 1)
-
-        @pl.when(j == R - 1)
+        @pl.when((j == R - 1) & (v < NV - DIRECT))
         def _():
             over_y(v)
 
-        chain(R // 2 - 2, over_near)
-        chain(R // 2, over_middle)
-        chain(R // 2 + 2, over_col)
+        @pl.when((j == R - 1) & (v >= NV - DIRECT))
+        def _():
+            over_rows(v)
+
+        for when, act in todo:
+            if when < NV * R:
+                pl.when(t == when)(act)
+        return carry
+
+    def own_starts():
         for q in range(PARTS):
-            at(P_FAR[q], lambda q=q: p_far(q).start())
-            at(P_NEAR, lambda q=q: near_arrives(q))
-
-            @pl.when(inner)
-            def _():
-                at(P_IN[q], lambda q=q: far_arrives(q))
-
-            @pl.when(jnp.logical_not(inner))
-            def _():
-                at(P_OUT[q], lambda q=q: far_arrives(q))
-        return carry
+            p_near(q).start()
+            all_across(z, q)
+
+    def near_comes():
+        for q in range(PARTS):
+            near_arrives(q)
+
+    def place(when):
+        return int(when * NV * R)
+
+    todo = [(place(OWN), own_starts), (place(NEAR), near_comes)]
+    for q in range(PARTS):
+        far = FAR[0] + (FAR[1] - FAR[0]) * q / max(PARTS - 1, 1)
+        todo.append((place(far), lambda q=q: p_far(q).start()))
+        todo.append((place(far + INTO), lambda q=q: pl.when(inner)(lambda: far_arrives(q))))
+        todo.append((place(far + INTO + ONWARD), lambda q=q: pl.when(jnp.logical_not(inner))(lambda: far_arrives(q))))
+    for v in range(NV - DIRECT):
+        for d, act in enumerate((over_near, over_middle, over_col)):
+            todo.append(((v + 1) * R - 1 + place(SUMS[d]), lambda v=v, act=act: act(v)))
+    todo.sort(key=lambda item: item[0])
 
     lax.fori_loop(0, NV * R, work, 0)
+    for when, act in todo:
+        if when >= NV * R:
+            act()
+    for v in range(NV - DIRECT, NV):
+        col_after_rows(v)
 
     for q in range(PARTS):
         for zo in range(Z):
@@ -344,12 +378,8 @@
         return carry
 
     lax.fori_loop(0, R, p_split, 0)
-    for v in range(NV - 1):
+    for v in range(NV):
         last_product(v)
-    over_near(NV - 1)
-    over_middle(NV - 1)
-    over_col(NV - 1)
-    last_product(NV - 1)
 
     for n in range(NJ):
         out[0, n] = total[0:B, n * L : n * L + B]
@@ -360,19 +390,26 @@
             return carry
 
         lax.fori_loop(0, R - 1, one, 0)
-        for i in range(1, Y):
-            for h in range(2):
-                y_copy(v, i, h).wait_send()
-        n_copy(v).wait_send()
-
-        @pl.when(inner)
-        def _():
-            for u in range(2):
-                c_copy(v, u).wait_send()
-
-        @pl.when(jnp.logical_not(inner))
-        def _():
-            f_copy(v).wait_send()
+        @pl.when(v < NV - DIRECT)
+        def _():
+            for i in range(1, Y):
+                for h in range(2):
+                    y_copy(v, i, h).wait_send()
+            n_copy(v).wait_send()
+
+            @pl.when(inner)
+            def _():
+                for u in range(2):
+                    c_copy(v, u).wait_send()
+
+            @pl.when(jnp.logical_not(inner))
+            def _():
+                f_copy(v).wait_send()
+
+        @pl.when(v >= NV - DIRECT)
+        def _():
+            for step in range(1, R):
+                m_copy(v, step).wait_send()
 
         for i in range(1, C):
             g_copy(v, i).wait_send()
@@ -428,6 +465,7 @@
             pltpu.VMEM((NV, 2, RV, L), f32),
             pltpu.VMEM((NV, RV, L), f32),
             pltpu.VMEM((NV, RV, L), f32),
+            pltpu.VMEM((max(DIRECT, 1), R, RV, L), f32),
             pltpu.VMEM((NV, C * RV, L), f32),
             pltpu.VMEM((L, C * RV), bf16),
             pltpu.VMEM((L, C * RV), bf16),
@@ -440,6 +478,7 @@
             dma((NV, Y, 2)), dma((NV, Y, 2)),
             dma((NV,)), dma((NV,)), dma((NV,)), dma((NV,)),
             dma((NV, 2)), dma((NV,)),
+            dma((max(DIRECT, 1), R)), dma((max(DIRECT, 1), R)),
             dma((NV, C)), dma((NV, C)),
             dma((PARTS,)), dma((PARTS,)), dma((2, PARTS)), dma((Z, Y, PARTS)), dma((R, PARTS)),
         ],

time: 119 us -> 96.2 us (0.81)
  Pallas kernels: 117 us -> 93.9 us
    pallas_call x1, Pallas kernels: 117 us -> 93.9 us  [shards(): pl.pallas_call(functools.partial(kernel, R, C, keep), out_shape=jax.Shape...]
where the time goes in v2:
time: 96.2 us; the launch traced here: 96 us
  Pallas kernels  93.9 us (98%)
  local copies, waits for them, and re-layouts  2.13 us (2%)
    pallas_call x1, Pallas kernels, shards(): pl.pallas_call(functools.partial(kernel, R, C, keep), out_shape=jax.Shape...  93.9 us
    pallas_call x1, local copies, waits for them, and re-layouts, shards(): pl.pallas_call(functools.partial(kernel, R, C, keep), out_shape=jax.Shape...  2.13 us

profile of v2, /device:TPU:0, one launch (start us, length us, event | category | flops | bytes accessed | tf_op | source)
XLA Modules:
  0.0 96.0 jit_solution(4926262143211984435)
XLA Ops:
  0.0 93.9 %shard_map.64 = f32[1,6,125,125]{3,2,1,0:T(8,128)} custom-call(f32[4000,125]{1,0:T(8,128)} %bitcast.9, f32[16,1000,125]{2,1,0:T(8,128)} %bitcast.8, f32[6,125,1,125]{3,2,1,0:T(1,128)} %bitcast.10, s32[128]{0:T(128)} %owner.1, s32[2,16]{1,0:T(2,128)} %bitcast.11, s32[1,6]{1,0:T(1,128)} %p_pat.1), custom_call_target="tpu_custom_call" | custom-call | tf_op jit(solution)/shard_map/pallas_call | solution.py:447
  93.9 2.1 %copy.7 = f32[1,6,125,125]{3,0,2,1:T(1,128)} copy(f32[1,6,125,125]{3,2,1,0:T(8,128)} %shard_map.64) | data formatting | bytes 750000 | tf_op jit(solution)/shard_map/pallas_call | solution.py:447

commit v3 on v2

--- a/solution.py
+++ b/solution.py
@@ -11,7 +11,7 @@
 Z = 4
 L = 128
 WAVES = 4
-PARTS = 3
+PARTS = 6
 WINDOW = 0.25
 DIRECT = 1
 MESH = pl.DeviceIdType.MESH
@@ -19,10 +19,11 @@
 
 SUMS = (0.2, 0.4, 0.6)
 OWN = 0.02
+LAST = 1.05
 NEAR = 0.3
-FAR = (0.25, 0.75)
+FAR = (0.05, 0.65)
 INTO = 0.31
-ONWARD = 0.12
+ONWARD = 0.15
 
 
 def split(v):
@@ -36,8 +37,8 @@
 
 
 def kernel(
-    R, C, KEEP, a_hbm, s_hbm, p_in, owner, a_pat, p_pat, out,
-    a_v, s_v, flip, asend, arecv, stage, sh, sl, ahl, macc, yrecv, nbuf, frecv, nrecv, crecv, mrecv,
+    R, C, KEEP, a_hbm, s_hbm, p_hbm, owner_hbm, a_pat_hbm, p_pat_hbm, out,
+    a_v, p_in, owner, a_pat, p_pat, s_v, flip, asend, arecv, stage, sh, sl, ahl, macc, yrecv, nbuf, frecv, nrecv, crecv, mrecv,
     mfull, mth, mtl, pbuf, ph, plo, total,
     load, a_s, a_r, y_s, y_r, f_s, f_r, n_s, n_r, c_s, c_r, m_s, m_r, g_s, g_r, pn_s, pf_s, pw_s, py_s, p_r,
 ):
@@ -57,7 +58,13 @@
 
     load_a = pltpu.make_async_copy(a_hbm, a_v, load.at[0])
     load_s = pltpu.make_async_copy(s_hbm, s_v, load.at[1])
+    small = [
+        pltpu.make_async_copy(src, dst, load.at[2 + i])
+        for i, (src, dst) in enumerate(((owner_hbm, owner), (a_pat_hbm, a_pat), (p_pat_hbm, p_pat), (p_hbm, p_in)))
+    ]
     load_a.start()
+    for c in small:
+        c.start()
     load_s.start()
 
     barrier = pltpu.get_barrier_semaphore()
@@ -79,11 +86,23 @@
         half = lax.div(j + 1, 2)
         return R // 2 + half * (1 - 2 * lax.rem(j, 2))
 
-    def a_copy(v, step):
-        return pltpu.make_async_remote_copy(
-            src_ref=asend.at[v, step], dst_ref=arecv.at[v, step], send_sem=a_s.at[v, step], recv_sem=a_r.at[v, step],
-            device_id={"row": lax.rem(me + step, R)}, device_id_type=MESH,
-        )
+    def a_copy(v, step, act):
+        def rows(count):
+            at = pl.ds(0, count)
+            act(pltpu.make_async_remote_copy(
+                src_ref=asend.at[v, step, :, at], dst_ref=arecv.at[v, step, :, at],
+                send_sem=a_s.at[v, step], recv_sem=a_r.at[v, step],
+                device_id={"row": lax.rem(me + step, R)}, device_id_type=MESH,
+            ))
+
+        @pl.when(lax.rem(v, H) == H - 1)
+        def _():
+            rows(B - (H - 1) * RV)
+
+        if H > 1:
+            @pl.when(lax.rem(v, H) != H - 1)
+            def _():
+                rows(RV)
 
     def pack(buf, step, k):
         rows, valid = pair(me, lax.rem(me + step, R))
@@ -98,7 +117,7 @@
     def p_copy(slot, q, target, s_sem):
         at = pl.ds(q * Q, Q)
         return pltpu.make_async_remote_copy(
-            src_ref=pbuf.at[slot, at], dst_ref=pbuf.at[slot, at], send_sem=s_sem, recv_sem=p_r.at[slot, q],
+            src_ref=pbuf.at[slot, at, pl.ds(0, B)], dst_ref=pbuf.at[slot, at, pl.ds(0, B)], send_sem=s_sem, recv_sem=p_r.at[slot, q],
             device_id={"row": target}, device_id_type=MESH,
         )
 
@@ -238,6 +257,12 @@
         total[...] += dot(mth[...], ph[v]) + (dot(mth[...], plo[v]) + dot(mtl[...], ph[v]))
 
     flip[...] = jnp.zeros_like(flip)
+    pad = H * RV - B
+    for k in range(KP):
+        arecv[k * H + H - 1, :, :, RV - pad : RV] = jnp.zeros((R, CAP, pad, L), f32)
+    pbuf[:, :, B:L] = jnp.zeros((R, NJ, L - B, L), f32)
+    for c in small:
+        c.wait()
     load_a.wait()
 
     def first_pack(j, carry):
@@ -248,7 +273,7 @@
     pl.semaphore_wait(barrier, R + C - 2)
 
     def send(n, carry):
-        a_copy(lax.div(n, R - 1), step_of(lax.rem(n, R - 1))).start()
+        a_copy(lax.div(n, R - 1), step_of(lax.rem(n, R - 1)), lambda c: c.start())
         return carry
 
     window = min(int(WINDOW * NV * R), H * (R - 1))
@@ -301,7 +326,7 @@
 
         @pl.when(j > 0)
         def _():
-            a_copy(v, step).wait_recv()
+            a_copy(v, step, lambda c: c.wait_recv())
             ahead = v * (R - 1) + j - 1 + window
 
             @pl.when(ahead < NV * (R - 1))
@@ -353,14 +378,14 @@
     for v in range(NV - DIRECT):
         for d, act in enumerate((over_near, over_middle, over_col)):
             todo.append(((v + 1) * R - 1 + place(SUMS[d]), lambda v=v, act=act: act(v)))
+    for v in range(NV - DIRECT, NV):
+        todo.append((max(place(LAST), NV * R), lambda v=v: col_after_rows(v)))
     todo.sort(key=lambda item: item[0])
 
     lax.fori_loop(0, NV * R, work, 0)
     for when, act in todo:
         if when >= NV * R:
             act()
-    for v in range(NV - DIRECT, NV):
-        col_after_rows(v)
 
     for q in range(PARTS):
         for zo in range(Z):
@@ -386,7 +411,7 @@
 
     def sent(v, carry):
         def one(j, carry):
-            a_copy(v, j + 1).wait_send()
+            a_copy(v, j + 1, lambda c: c.wait_send())
             return carry
 
         lax.fori_loop(0, R - 1, one, 0)
@@ -442,15 +467,18 @@
     slab = prolong_slab.transpose(0, 2, 1, 3).reshape(W, B * NA, B)
     dma = pltpu.SemaphoreType.DMA
     vmem = pl.BlockSpec(memory_space=pltpu.VMEM)
-    smem = pl.BlockSpec(memory_space=pltpu.SMEM)
     hbm = pl.BlockSpec(memory_space=pl.ANY)
     return pl.pallas_call(
         functools.partial(kernel, R, C, keep),
         out_shape=jax.ShapeDtypeStruct((1, NJ, B, B), f32),
-        in_specs=[hbm, hbm, vmem, smem, smem, smem],
+        in_specs=[hbm] * 6,
         out_specs=vmem,
         scratch_shapes=[
             pltpu.VMEM((W * B * KP, B), f32),
+            pltpu.VMEM((NJ, B, 1, B), f32),
+            pltpu.SMEM(row_owner.shape, jnp.int32),
+            pltpu.SMEM((KP, W), jnp.int32),
+            pltpu.SMEM((1, NJ), jnp.int32),
             pltpu.VMEM((W, B * NA, B), f32),
             pltpu.VMEM((CAP, L, L), f32),
             pltpu.VMEM((NV, R, CAP, RV, L), f32),
@@ -473,7 +501,7 @@
             pltpu.VMEM((NV, C * RV, NJ * L), bf16),
             pltpu.VMEM((NV, C * RV, NJ * L), bf16),
             pltpu.VMEM((L, NJ * L), f32),
-            dma((2,)),
+            dma((6,)),
             dma((NV, R)), dma((NV, R)),
             dma((NV, Y, 2)), dma((NV, Y, 2)),
             dma((NV,)), dma((NV,)), dma((NV,)), dma((NV,)),

time: 96.2 us -> 90.9 us (0.945)
  Pallas kernels: 93.9 us -> 88.6 us
    pallas_call x1, Pallas kernels: 93.9 us -> 88.6 us  [shards(): pl.pallas_call(functools.partial(kernel, R, C, keep), out_shape=jax.Shape...]
where the time goes in v3:
time: 90.9 us; the launch traced here: 90.8 us
  Pallas kernels  88.6 us (97%)
  local copies, waits for them, and re-layouts  2.13 us (2%)
    pallas_call x1, Pallas kernels, shards(): pl.pallas_call(functools.partial(kernel, R, C, keep), out_shape=jax.Shape...  88.6 us
    pallas_call x1, local copies, waits for them, and re-layouts, shards(): pl.pallas_call(functools.partial(kernel, R, C, keep), out_shape=jax.Shape...  2.13 us

profile of v3, /device:TPU:0, one launch (start us, length us, event | category | flops | bytes accessed | tf_op | source)
XLA Modules:
  0.0 90.8 jit_solution(3317791642716037113)
XLA Ops:
  0.0 88.6 %shard_map.64 = f32[1,6,125,125]{3,2,1,0:T(8,128)} custom-call(f32[4000,125]{1,0:T(8,128)} %bitcast.9, f32[16,1000,125]{2,1,0:T(8,128)} %bitcast.8, f32[6,125,1,125]{3,2,1,0:T(1,128)} %bitcast.10, s32[128]{0:T(128)} %owner_hbm.1, s32[2,16]{1,0:T(2,128)} %bitcast.11, s32[1,6]{1,0:T(1,128)} %p_pat_hbm.1), custom_call_target="tpu_custom_call" | custom-call | tf_op jit(solution)/shard_map/pallas_call | solution.py:471
  88.6 2.1 %copy.7 = f32[1,6,125,125]{3,0,2,1:T(1,128)} copy(f32[1,6,125,125]{3,2,1,0:T(8,128)} %shard_map.64) | data formatting | bytes 750000 | tf_op jit(solution)/shard_map/pallas_call | solution.py:471

commit v4 on v3

--- a/solution.py
+++ b/solution.py
@@ -10,10 +10,12 @@
 CAP = 2
 Z = 4
 L = 128
-WAVES = 4
+CUTS = (128,)
+SMALL_CUTS = (64, 64)
+LAST_CUTS = (64, 64)
 PARTS = 6
-WINDOW = 0.25
-DIRECT = 1
+WINDOW = (6, 10, 12)
+DIRECT = 0
 MESH = pl.DeviceIdType.MESH
 VMEM_LIMIT = 58 * 1024 * 1024
 
@@ -21,9 +23,19 @@
 OWN = 0.02
 LAST = 1.05
 NEAR = 0.3
-FAR = (0.05, 0.65)
+FAR = (0.05, 0.75)
 INTO = 0.31
 ONWARD = 0.15
+
+
+def waves_of(KP, roomy):
+    waves = []
+    for k in range(KP):
+        first = 0
+        for rows in LAST_CUTS if k == KP - 1 else CUTS if roomy else SMALL_CUTS:
+            waves.append((k, first, rows))
+            first += rows
+    return waves
 
 
 def split(v):
@@ -44,8 +56,9 @@
 ):
     KP, W, B = a_pat.shape[0], a_pat.shape[1], a_v.shape[1]
     NA, NJ = s_v.shape[1] // B, p_in.shape[0]
-    NV, RV = WAVES, KP * L // WAVES
-    H, Q = L // RV, NJ // PARTS
+    waves = waves_of(KP, KEEP)
+    NV, Q = len(waves), NJ // PARTS
+    window = [WINDOW[min(v, len(WINDOW) - 1)] * R // 8 for v in range(NV)]
     Y = R // Z
     f32 = jnp.float32
     me, col = lax.axis_index("row"), lax.axis_index("col")
@@ -86,33 +99,24 @@
         half = lax.div(j + 1, 2)
         return R // 2 + half * (1 - 2 * lax.rem(j, 2))
 
-    def a_copy(v, step, act):
-        def rows(count):
-            at = pl.ds(0, count)
-            act(pltpu.make_async_remote_copy(
-                src_ref=asend.at[v, step, :, at], dst_ref=arecv.at[v, step, :, at],
-                send_sem=a_s.at[v, step], recv_sem=a_r.at[v, step],
-                device_id={"row": lax.rem(me + step, R)}, device_id_type=MESH,
-            ))
-
-        @pl.when(lax.rem(v, H) == H - 1)
-        def _():
-            rows(B - (H - 1) * RV)
-
-        if H > 1:
-            @pl.when(lax.rem(v, H) != H - 1)
-            def _():
-                rows(RV)
+    def a_copy(v, step):
+        at = pl.ds(0, min(waves[v][2], B - waves[v][1]))
+        return pltpu.make_async_remote_copy(
+            src_ref=asend.at[v, step, :, at], dst_ref=arecv.at[v, step, :, at],
+            send_sem=a_s.at[v, step], recv_sem=a_r.at[v, step],
+            device_id={"row": lax.rem(me + step, R)}, device_id_type=MESH,
+        )
 
     def pack(buf, step, k):
-        rows, valid = pair(me, lax.rem(me + step, R))
+        chosen, valid = pair(me, lax.rem(me + step, R))
         for s in range(CAP):
-            scale = jnp.where(valid, a_pat[k, rows[s]], 0).astype(f32)
-            flip[s, 0:B, 0:B] = a_v[pl.ds(rows[s] * (B * KP) + k, B, stride=KP), :] * scale
+            scale = jnp.where(valid, a_pat[k, chosen[s]], 0).astype(f32)
+            flip[s, 0:B, 0:B] = a_v[pl.ds(chosen[s] * (B * KP) + k, B, stride=KP), :] * scale
         for s in range(CAP):
             turned = flip[s].T
-            for h in range(H):
-                buf[k * H + h, step, s] = turned[h * RV : (h + 1) * RV]
+            for v, (block, first, rows) in enumerate(waves):
+                if block == k:
+                    buf[v, step, s, 0:rows] = turned[first : first + rows]
 
     def p_copy(slot, q, target, s_sem):
         at = pl.ds(q * Q, Q)
@@ -154,34 +158,41 @@
 
             all_across(far0 + u, q)
 
+    def tall(v):
+        return pl.ds(0, waves[v][2])
+
+    def mine(v):
+        rows = waves[v][2]
+        return pl.ds(pl.multiple_of(col * rows, rows), rows)
+
     def y_copy(v, i, h):
         target = lax.rem(y + i, Y)
         at = pl.ds(near0 if h else far0, 2)
         return pltpu.make_async_remote_copy(
-            src_ref=macc.at[v, target, at], dst_ref=yrecv.at[v, i, at], send_sem=y_s.at[v, i, h], recv_sem=y_r.at[v, i, h],
+            src_ref=macc.at[v, target, at, tall(v)], dst_ref=yrecv.at[v, i, at, tall(v)], send_sem=y_s.at[v, i, h], recv_sem=y_r.at[v, i, h],
             device_id={"row": z * Y + target}, device_id_type=MESH,
         )
 
     def f_copy(v):
         return pltpu.make_async_remote_copy(
-            src_ref=nbuf.at[v, pl.ds(far0, 2)], dst_ref=frecv.at[v], send_sem=f_s.at[v], recv_sem=f_r.at[v],
+            src_ref=nbuf.at[v, pl.ds(far0, 2), tall(v)], dst_ref=frecv.at[v, :, tall(v)], send_sem=f_s.at[v], recv_sem=f_r.at[v],
             device_id={"row": zn * Y + y}, device_id_type=MESH,
         )
 
     def n_copy(v):
         return pltpu.make_async_remote_copy(
-            src_ref=nbuf.at[v, zn], dst_ref=nrecv.at[v], send_sem=n_s.at[v], recv_sem=n_r.at[v],
+            src_ref=nbuf.at[v, zn, tall(v)], dst_ref=nrecv.at[v, tall(v)], send_sem=n_s.at[v], recv_sem=n_r.at[v],
             device_id={"row": zn * Y + y}, device_id_type=MESH,
         )
 
     def c_copy(v, u):
         return pltpu.make_async_remote_copy(
-            src_ref=nbuf.at[v, far0 + u], dst_ref=crecv.at[v], send_sem=c_s.at[v, u], recv_sem=c_r.at[v],
+            src_ref=nbuf.at[v, far0 + u, tall(v)], dst_ref=crecv.at[v, tall(v)], send_sem=c_s.at[v, u], recv_sem=c_r.at[v],
             device_id={"row": (far0 + u) * Y + y}, device_id_type=MESH,
         )
 
     def g_copy(v, i):
-        at = pl.ds(pl.multiple_of(col * RV, RV), RV)
+        at = mine(v)
         return pltpu.make_async_remote_copy(
             src_ref=mfull.at[v, at], dst_ref=mfull.at[v, at], send_sem=g_s.at[v, i], recv_sem=g_r.at[v, i],
             device_id={"col": lax.rem(col + i, C)}, device_id_type=MESH,
@@ -195,11 +206,11 @@
     def over_near(v):
         for h in range(2):
             at = pl.ds(near0 if h else far0, 2)
-            acc = macc[v, y, at]
+            acc = macc[v, y, at, tall(v)]
             for i in range(1, Y):
                 y_copy(v, i, h).wait_recv()
-                acc += yrecv[v, i, at]
-            nbuf[v, at] = acc
+                acc += yrecv[v, i, at, tall(v)]
+            nbuf[v, at, tall(v)] = acc
             if h == 0:
                 @pl.when(jnp.logical_not(inner))
                 def _():
@@ -211,22 +222,22 @@
         @pl.when(inner)
         def _():
             f_copy(v).wait_recv()
-            nbuf[v, pl.ds(far0, 2)] += frecv[v]
+            nbuf[v, pl.ds(far0, 2), tall(v)] += frecv[v, :, tall(v)]
             for u in range(2):
                 c_copy(v, u).start()
 
     def over_col(v):
         n_copy(v).wait_recv()
         c_copy(v, 0).wait_recv()
-        mfull[v, pl.ds(pl.multiple_of(col * RV, RV), RV)] = nbuf[v, z] + nrecv[v] + crecv[v]
+        mfull[v, mine(v)] = nbuf[v, z, tall(v)] + nrecv[v, tall(v)] + crecv[v, tall(v)]
         for i in range(1, C):
             g_copy(v, i).start()
 
     def m_copy(v, step):
         target = lax.rem(me + step, R)
-        d = jnp.maximum(v - (NV - DIRECT), 0)
-        return pltpu.make_async_remote_copy(
-            src_ref=macc.at[v, lax.rem(target, Y), lax.div(target, Y)], dst_ref=mrecv.at[d, step],
+        d = v - (NV - DIRECT)
+        return pltpu.make_async_remote_copy(
+            src_ref=macc.at[v, lax.rem(target, Y), lax.div(target, Y), tall(v)], dst_ref=mrecv.at[d, step, tall(v)],
             send_sem=m_s.at[d, step], recv_sem=m_r.at[d, step],
             device_id={"row": target}, device_id_type=MESH,
         )
@@ -239,27 +250,29 @@
         lax.fori_loop(0, R - 1, one, 0)
 
     def col_after_rows(v):
-        acc = macc[v, y, z]
+        acc = macc[v, y, z, tall(v)]
         for step in range(1, R):
             m_copy(v, step).wait_recv()
-            acc += mrecv[v - (NV - DIRECT), step]
-        mfull[v, pl.ds(pl.multiple_of(col * RV, RV), RV)] = acc
+            acc += mrecv[v - (NV - DIRECT), step, tall(v)]
+        mfull[v, mine(v)] = acc
         for i in range(1, C):
             g_copy(v, i).start()
 
     def last_product(v):
         for i in range(1, C):
             g_copy(v, i).wait_recv()
-        for c in range(C * RV // L):
+        width = C * waves[v][2]
+        for c in range(width // L):
             hi, lo = split(mfull[v, c * L : (c + 1) * L].T)
             mth[:, c * L : (c + 1) * L] = hi
             mtl[:, c * L : (c + 1) * L] = lo
-        total[...] += dot(mth[...], ph[v]) + (dot(mth[...], plo[v]) + dot(mtl[...], ph[v]))
+        mh, ml, fh = mth[:, 0:width], mtl[:, 0:width], ph[v, 0:width]
+        total[...] += dot(mh, fh) + (dot(mh, plo[v, 0:width]) + dot(ml, fh))
 
     flip[...] = jnp.zeros_like(flip)
-    pad = H * RV - B
-    for k in range(KP):
-        arecv[k * H + H - 1, :, :, RV - pad : RV] = jnp.zeros((R, CAP, pad, L), f32)
+    for v, (block, first, rows) in enumerate(waves):
+        if first + rows > B:
+            arecv[v, :, :, B - first : rows] = jnp.zeros((R, CAP, first + rows - B, L), f32)
     pbuf[:, :, B:L] = jnp.zeros((R, NJ, L - B, L), f32)
     for c in small:
         c.wait()
@@ -272,12 +285,12 @@
     lax.fori_loop(0, R - 1, first_pack, 0)
     pl.semaphore_wait(barrier, R + C - 2)
 
-    def send(n, carry):
-        a_copy(lax.div(n, R - 1), step_of(lax.rem(n, R - 1)), lambda c: c.start())
-        return carry
-
-    window = min(int(WINDOW * NV * R), H * (R - 1))
-    lax.fori_loop(0, window, send, 0)
+    def send(n):
+        if n < NV * (R - 1):
+            a_copy(n // (R - 1), step_of(jnp.int32(n % (R - 1)))).start()
+
+    for n in range(window[0]):
+        send(n)
 
     for k in range(1, KP):
         def later_pack(j, carry):
@@ -313,48 +326,41 @@
 
             lax.fori_loop(0, NA // 2, one, 0)
 
-    def work(t, carry):
-        v, j = lax.div(t, R), lax.rem(t, R)
+    def work(v, j, carry):
+        rows = waves[v][2]
         step = jnp.where(j == 0, 0, step_of(j - 1))
         keep = step if KEEP else 0
-        if KEEP:
-            @pl.when(v == 0)
-            def _():
-                slab(step, step)
-        else:
-            slab(step, 0)
+        if v == 0 or not KEEP:
+            slab(step, keep)
 
         @pl.when(j > 0)
         def _():
-            a_copy(v, step, lambda c: c.wait_recv())
-            ahead = v * (R - 1) + j - 1 + window
-
-            @pl.when(ahead < NV * (R - 1))
-            def _():
-                send(ahead, 0)
+            a_copy(v, step).wait_recv()
+            for other in range(v, NV):
+                ahead = j - 1 + window[v] - (other - v) * (R - 1)
+
+                @pl.when((ahead >= 0) & (ahead < R - 1))
+                def _():
+                    a_copy(other, step_of(ahead)).start()
 
         for s in range(CAP):
-            hi, lo = split(arecv[v, step, s])
-            ahl[0:RV, s * L : (s + 1) * L] = hi
-            ahl[RV : 2 * RV, s * L : (s + 1) * L] = lo
+            hi, lo = split(arecv[v, step, s, tall(v)])
+            ahl[0:rows, s * L : (s + 1) * L] = hi
+            ahl[rows : 2 * rows, s * L : (s + 1) * L] = lo
         for b in range(NA // 2):
-            both = dot(ahl[...], sh[keep, b])
-            r = both[0:RV] + (both[RV : 2 * RV] + dot(ahl[0:RV], sl[keep, b]))
+            both = dot(ahl[0 : 2 * rows], sh[keep, b])
+            r = both[0:rows] + (both[rows : 2 * rows] + dot(ahl[0:rows], sl[keep, b]))
             for h in range(2):
                 a = 2 * b + h
-                macc[v, a % Y, a // Y] += r[:, h * L : (h + 1) * L]
-
-        @pl.when((j == R - 1) & (v < NV - DIRECT))
+                macc[v, a % Y, a // Y, tall(v)] += r[:, h * L : (h + 1) * L]
+
+        @pl.when(j == R - 1)
         def _():
-            over_y(v)
-
-        @pl.when((j == R - 1) & (v >= NV - DIRECT))
-        def _():
-            over_rows(v)
+            (over_y if v < NV - DIRECT else over_rows)(v)
 
         for when, act in todo:
-            if when < NV * R:
-                pl.when(t == when)(act)
+            if when // R == v:
+                pl.when(j == when % R)(act)
         return carry
 
     def own_starts():
@@ -366,8 +372,16 @@
         for q in range(PARTS):
             near_arrives(q)
 
+    ends = []
+    for v, (_, _, rows) in enumerate(waves):
+        start = ends[-1] if ends else 0.0
+        ends += [start + rows * (j + 1) / (R * KP * L) for j in range(R)]
+
     def place(when):
-        return int(when * NV * R)
+        for t, end in enumerate(ends):
+            if when <= end:
+                return t
+        return NV * R + int((when - 1) * 1000)
 
     todo = [(place(OWN), own_starts), (place(NEAR), near_comes)]
     for q in range(PARTS):
@@ -377,12 +391,16 @@
         todo.append((place(far + INTO + ONWARD), lambda q=q: pl.when(jnp.logical_not(inner))(lambda: far_arrives(q))))
     for v in range(NV - DIRECT):
         for d, act in enumerate((over_near, over_middle, over_col)):
-            todo.append(((v + 1) * R - 1 + place(SUMS[d]), lambda v=v, act=act: act(v)))
+            todo.append((place(ends[(v + 1) * R - 1] + SUMS[d]), lambda v=v, act=act: act(v)))
     for v in range(NV - DIRECT, NV):
         todo.append((max(place(LAST), NV * R), lambda v=v: col_after_rows(v)))
     todo.sort(key=lambda item: item[0])
 
-    lax.fori_loop(0, NV * R, work, 0)
+    for v in range(NV):
+        if v > 0:
+            for n in range(window[v - 1], window[v]):
+                send(v * (R - 1) + n)
+        lax.fori_loop(0, R, functools.partial(work, v), 0)
     for when, act in todo:
         if when >= NV * R:
             act()
@@ -392,31 +410,31 @@
             for i in range(1, Y):
                 p_arrived(zo * Y + lax.rem(y + i, Y), q)
 
-    def p_split(r, carry):
-        c, k = lax.div(r, KP), lax.rem(r, KP)
-        at = pl.ds(pl.multiple_of(c * RV, RV), RV)
-        for n in range(NJ):
-            hi, lo = split(pbuf[r, n])
-            for h in range(H):
-                ph[k * H + h, at, n * L : (n + 1) * L] = hi[h * RV : (h + 1) * RV]
-                plo[k * H + h, at, n * L : (n + 1) * L] = lo[h * RV : (h + 1) * RV]
+    def p_split(c, carry):
+        for k in range(KP):
+            for n in range(NJ):
+                hi, lo = split(pbuf[c * KP + k, n])
+                for v, (block, first, rows) in enumerate(waves):
+                    if block == k:
+                        at = pl.ds(pl.multiple_of(c * rows, rows), rows)
+                        ph[v, at, n * L : (n + 1) * L] = hi[first : first + rows]
+                        plo[v, at, n * L : (n + 1) * L] = lo[first : first + rows]
         return carry
 
-    lax.fori_loop(0, R, p_split, 0)
+    lax.fori_loop(0, C, p_split, 0)
     for v in range(NV):
         last_product(v)
 
     for n in range(NJ):
         out[0, n] = total[0:B, n * L : n * L + B]
 
-    def sent(v, carry):
-        def one(j, carry):
-            a_copy(v, j + 1, lambda c: c.wait_send())
+    for v in range(NV):
+        def sent(j, carry):
+            a_copy(v, j + 1).wait_send()
             return carry
 
-        lax.fori_loop(0, R - 1, one, 0)
-        @pl.when(v < NV - DIRECT)
-        def _():
+        lax.fori_loop(0, R - 1, sent, 0)
+        if v < NV - DIRECT:
             for i in range(1, Y):
                 for h in range(2):
                     y_copy(v, i, h).wait_send()
@@ -430,17 +448,11 @@
             @pl.when(jnp.logical_not(inner))
             def _():
                 f_copy(v).wait_send()
-
-        @pl.when(v >= NV - DIRECT)
-        def _():
+        else:
             for step in range(1, R):
                 m_copy(v, step).wait_send()
-
         for i in range(1, C):
             g_copy(v, i).wait_send()
-        return carry
-
-    lax.fori_loop(0, NV, sent, 0)
     for q in range(PARTS):
         p_near(q).wait_send()
         p_far(q).wait_send()
@@ -460,8 +472,9 @@
     W, KP, B = a_blocks.shape[:3]
     NA, NJ = prolong_slab.shape[1], prolong.shape[1]
     f32, bf16 = jnp.float32, jnp.bfloat16
-    Y, NV, RV = R // Z, WAVES, KP * L // WAVES
     keep = R * NA <= 64
+    waves = waves_of(KP, keep)
+    Y, NV, RV = R // Z, len(waves), max(rows for _, _, rows in waves)
     slots = R if keep else 1
     oper = a_blocks.transpose(0, 2, 1, 3).reshape(W * B * KP, B)
     slab = prolong_slab.transpose(0, 2, 1, 3).reshape(W, B * NA, B)

time: 90.9 us -> 88.3 us (0.971)
  Pallas kernels: 88.6 us -> 86 us
    pallas_call x1, Pallas kernels: 88.6 us -> 86 us  [shards(): pl.pallas_call(functools.partial(kernel, R, C, keep), out_shape=jax.Shape...]
where the time goes in v4:
time: 88.3 us; the launch traced here: 88.2 us
  Pallas kernels  86 us (97%)
  local copies, waits for them, and re-layouts  2.13 us (2%)
    pallas_call x1, Pallas kernels, shards(): pl.pallas_call(functools.partial(kernel, R, C, keep), out_shape=jax.Shape...  86 us
    pallas_call x1, local copies, waits for them, and re-layouts, shards(): pl.pallas_call(functools.partial(kernel, R, C, keep), out_shape=jax.Shape...  2.13 us

profile of v4, /device:TPU:0, one launch (start us, length us, event | category | flops | bytes accessed | tf_op | source)
XLA Modules:
  0.0 88.2 jit_solution(17566102523090336352)
XLA Ops:
  0.0 86.0 %shard_map.64 = f32[1,6,125,125]{3,2,1,0:T(8,128)} custom-call(f32[4000,125]{1,0:T(8,128)} %bitcast.9, f32[16,1000,125]{2,1,0:T(8,128)} %bitcast.8, f32[6,125,1,125]{3,2,1,0:T(1,128)} %bitcast.10, s32[128]{0:T(128)} %owner_hbm.1, s32[2,16]{1,0:T(2,128)} %bitcast.11, s32[1,6]{1,0:T(1,128)} %p_pat_hbm.1), custom_call_target="tpu_custom_call" | custom-call | tf_op jit(solution)/shard_map/pallas_call | solution.py:484
  86.1 2.1 %copy.7 = f32[1,6,125,125]{3,0,2,1:T(1,128)} copy(f32[1,6,125,125]{3,2,1,0:T(8,128)} %shard_map.64) | data formatting | bytes 750000 | tf_op jit(solution)/shard_map/pallas_call | solution.py:484

commit v5 on v4

--- a/solution.py
+++ b/solution.py
@@ -14,7 +14,7 @@
 SMALL_CUTS = (64, 64)
 LAST_CUTS = (64, 64)
 PARTS = 6
-WINDOW = (6, 10, 12)
+WINDOW = (7, 12, 14)
 DIRECT = 0
 MESH = pl.DeviceIdType.MESH
 VMEM_LIMIT = 58 * 1024 * 1024
@@ -69,7 +69,7 @@
     inner = (z == 1) | (z == 2)
     far_inner = jnp.where(z < 2, 2, 1)
 
-    load_a = pltpu.make_async_copy(a_hbm, a_v, load.at[0])
+    load_a = pltpu.make_async_copy(a_hbm, a_v.at[pl.ds(0, W * B * KP)], load.at[0])
     load_s = pltpu.make_async_copy(s_hbm, s_v, load.at[1])
     small = [
         pltpu.make_async_copy(src, dst, load.at[2 + i])
@@ -410,18 +410,19 @@
             for i in range(1, Y):
                 p_arrived(zo * Y + lax.rem(y + i, Y), q)
 
-    def p_split(c, carry):
+    def p_split(i, carry):
+        c, n = lax.div(i, NJ), lax.rem(i, NJ)
+        lanes = pl.ds(pl.multiple_of(n * L, L), L)
         for k in range(KP):
-            for n in range(NJ):
-                hi, lo = split(pbuf[c * KP + k, n])
-                for v, (block, first, rows) in enumerate(waves):
-                    if block == k:
-                        at = pl.ds(pl.multiple_of(c * rows, rows), rows)
-                        ph[v, at, n * L : (n + 1) * L] = hi[first : first + rows]
-                        plo[v, at, n * L : (n + 1) * L] = lo[first : first + rows]
+            hi, lo = split(pbuf[c * KP + k, n])
+            for v, (block, first, rows) in enumerate(waves):
+                if block == k:
+                    at = pl.ds(pl.multiple_of(c * rows, rows), rows)
+                    ph[v, at, lanes] = hi[first : first + rows]
+                    plo[v, at, lanes] = lo[first : first + rows]
         return carry
 
-    lax.fori_loop(0, C, p_split, 0)
+    lax.fori_loop(0, C * NJ, p_split, 0)
     for v in range(NV):
         last_product(v)
 
@@ -487,7 +488,7 @@
         in_specs=[hbm] * 6,
         out_specs=vmem,
         scratch_shapes=[
-            pltpu.VMEM((W * B * KP, B), f32),
+            pltpu.VMEM((W * B * KP + 8, B), f32),
             pltpu.VMEM((NJ, B, 1, B), f32),
             pltpu.SMEM(row_owner.shape, jnp.int32),
             pltpu.SMEM((KP, W), jnp.int32),

time: 88.3 us -> 88.2 us (level)
  no operation moved by 1% of the time
where the time goes in v5:
time: 88.2 us; the launch traced here: 88.1 us
  Pallas kernels  85.9 us (97%)
  local copies, waits for them, and re-layouts  2.13 us (2%)
    pallas_call x1, Pallas kernels, shards(): pl.pallas_call(functools.partial(kernel, R, C, keep), out_shape=jax.Shape...  85.9 us
    pallas_call x1, local copies, waits for them, and re-layouts, shards(): pl.pallas_call(functools.partial(kernel, R, C, keep), out_shape=jax.Shape...  2.13 us

profile of v5, /device:TPU:0, one launch (start us, length us, event | category | flops | bytes accessed | tf_op | source)
XLA Modules:
  0.0 88.1 jit_solution(15352454060109012912)
XLA Ops:
  0.0 85.9 %shard_map.64 = f32[1,6,125,125]{3,2,1,0:T(8,128)} custom-call(f32[4000,125]{1,0:T(8,128)} %bitcast.9, f32[16,1000,125]{2,1,0:T(8,128)} %bitcast.8, f32[6,125,1,125]{3,2,1,0:T(1,128)} %bitcast.10, s32[128]{0:T(128)} %owner_hbm.1, s32[2,16]{1,0:T(2,128)} %bitcast.11, s32[1,6]{1,0:T(1,128)} %p_pat_hbm.1), custom_call_target="tpu_custom_call" | custom-call | tf_op jit(solution)/shard_map/pallas_call | solution.py:485
  85.9 2.1 %copy.7 = f32[1,6,125,125]{3,0,2,1:T(1,128)} copy(f32[1,6,125,125]{3,2,1,0:T(8,128)} %shard_map.64) | data formatting | bytes 750000 | tf_op jit(solution)/shard_map/pallas_call | solution.py:485
